TPU v7x, 32 devices: a whole 2x2x4 slice. The times are simulated.
32 devices in a mesh: dp: 8 (over z, x), sp: 4 (over y, core).
Axes of the slice: x: 2, y: 2, z: 4, core: 2. Of those that a mesh axis runs over, the one named last changes fastest.
Arguments:
- base_query: bfloat16 [8, 1024, 4096], P('dp', 'sp'), may hold values from -8 to 8
- base_key: bfloat16 [8, 1024, 512], P('dp', 'sp'), may hold values from -8 to 8
- reference_value_rows: bfloat16 [8, 1024, 512], P('dp', 'sp'), may hold values from -6 to 6
- actor_query: bfloat16 [8, 1024, 4096], P('dp', 'sp'), may hold values from -8 to 8
- actor_key: bfloat16 [8, 1024, 512], P('dp', 'sp'), may hold values from -8 to 8
- actor_value_rows: bfloat16 [8, 1024, 512], P('dp', 'sp'), may hold values from -6 to 6
- segment_labels: int32 [8, 1024], P('dp', 'sp'), may hold values from 0 to 2, never falling along the last dimension, each value on 1 to 512 neighbouring positions
- shard_plan: int32 [8], replicated, may hold values from 0 to 7, each once
Outputs:
- base_output: bfloat16 [8, 1024, 4096], P('dp', 'sp')
- actor_output: bfloat16 [8, 1024, 4096], P('dp', 'sp')
Inputs may be any that keep to these rules, and one draw needn't show every extreme that they name: `segment_labels`: along an owner's rows the labels never decrease; a response has 1 to 512 rows, and some response has exactly 512. `shard_plan`: each group is named by exactly one owner.
All inputs are finite; a program needn't handle non-finite values.
Results may differ from a plain program's by a relative error of at most 0.0079.
Values may be sent and summed in bfloat16 or wider, within the bound.
A program may use at most 128 MiB of HBM per device.

v0:
```python
import functools
import math

import jax
import jax.numpy as jnp
import numpy as np
from jax import lax
from jax.experimental import pallas as pl
from jax.experimental.pallas import tpu as pltpu
from jax.sharding import PartitionSpec as P

QUERY_HEADS = 32
KEY_VALUE_HEADS = 4
HEAD_SIZE = 128
GROUP = QUERY_HEADS // KEY_VALUE_HEADS
THETA = 1000000.0
MESH = pl.DeviceIdType.MESH
BF16 = jnp.bfloat16
F32 = jnp.float32


def kernel(
    owners, members, rows, tile, cap,
    plan_ref, lab_ref, rate_ref, bq_hbm, bk_hbm, bv_hbm, aq_hbm, ak_hbm, av_hbm,
    base_out, actor_out,
    labs, cs, sn, bias, qs, ks, kx, vx, att, land, fwd, bo, out_box, in_box,
    q_sem, k_sem, v_sem,
    lab_send, lab_recv, k_send, v_send, k_recv, v_recv,
    one_send, one_recv, two_send, two_recv, bo_sem, box_send, box_recv,
):
    D = HEAD_SIZE
    me = lax.axis_index("dp")
    s = lax.axis_index("sp")
    back = 2 * rows
    span = 3 * rows
    splits = owners // GROUP
    part = rows // splits

    loads = {}
    for p, q_hbm, k_hbm, v_hbm in ((1, aq_hbm, ak_hbm, av_hbm), (0, bq_hbm, bk_hbm, bv_hbm)):
        loads[p] = (
            pltpu.make_async_copy(q_hbm, qs.at[p], q_sem.at[p]),
            pltpu.make_async_copy(k_hbm, ks.at[p], k_sem.at[p]),
            pltpu.make_async_copy(v_hbm, vx.at[p, pl.ds(back, rows), :], v_sem.at[p]),
        )
    for p in (1, 0):
        for load in (loads[p][2], loads[p][1], loads[p][0]):
            load.start()

    def col(h):
        return pl.ds(pl.multiple_of(h * D, D), D)

    labs[2] = jnp.broadcast_to(lab_ref[...], labs.shape[1:])
    barrier = pltpu.get_barrier_semaphore()

    def greet_owner(j, c):
        pl.semaphore_signal(
            barrier, inc=1, device_id={"dp": lax.rem(me + j, owners)}, device_id_type=MESH
        )
        return c

    lax.fori_loop(1, owners, greet_owner, 0)
    for j in range(1, members):
        pl.semaphore_signal(
            barrier, inc=1, device_id={"sp": lax.rem(s + j, members)}, device_id_type=MESH
        )
    pl.semaphore_wait(barrier, owners - 1 + members - 1)

    def to_later(src, dst_of, send_sem, recv_sem):
        for step in (1, 2):
            pltpu.make_async_remote_copy(
                src_ref=src,
                dst_ref=dst_of(2 - step),
                send_sem=send_sem,
                recv_sem=recv_sem,
                device_id={"sp": lax.rem(s + step, members)},
                device_id_type=MESH,
            ).start()

    def send_key(p, h):
        to_later(
            kx.at[p, pl.ds(back, rows), col(h)],
            lambda slot: kx.at[p, pl.ds(slot * rows, rows), col(h)],
            k_send.at[p], k_recv.at[p, h],
        )

    def send_value(p, h):
        to_later(
            vx.at[p, pl.ds(back, rows), col(h)],
            lambda slot: vx.at[p, pl.ds(slot * rows, rows), col(h)],
            v_send.at[p], v_recv.at[p, h],
        )

    to_later(labs.at[2], lambda slot: labs.at[slot], lab_send, lab_recv)
    loads[1][2].wait()
    send_value(1, 0)
    pltpu.make_async_copy(labs.at[pl.ds(0, 2)], labs.at[pl.ds(0, 2)], lab_recv).wait()

    lab_row = jnp.concatenate([labs[0, :1, :], labs[1, :1, :], labs[2, :1, :]], axis=1).astype(F32)
    place = lax.broadcasted_iota(jnp.int32, (1, span), 1)
    lab_row = jnp.where(place + (s - 2) * rows >= 0, lab_row, -1.0)
    own = lab_row[:, back:]
    r_id = lax.broadcasted_iota(jnp.int32, (rows, rows), 0)
    c_id = lax.broadcasted_iota(jnp.int32, (rows, rows), 1)
    lab_col = jnp.sum(jnp.where(r_id == c_id, own, 0.0), axis=1, keepdims=True)
    begin = jnp.sum(jnp.where(lab_row < lab_col, 1.0, 0.0), axis=1, keepdims=True)
    r_place = lax.broadcasted_iota(jnp.int32, (rows, 1), 0) + back
    positions = r_place.astype(F32) - begin
    angles = positions * rate_ref[:1, :]
    lane = lax.broadcasted_iota(jnp.int32, (rows, D), 1)
    cs[...] = jnp.cos(angles)
    sine = jnp.sin(angles)
    sn[...] = jnp.where(lane < D // 2, -sine, sine)
    wide = lax.broadcasted_iota(jnp.int32, (rows, span), 1)
    row_of = lax.broadcasted_iota(jnp.int32, (rows, span), 0) + back
    allowed = jnp.where(wide <= row_of, jnp.where(lab_row == lab_col, 0.0, -1e30), -1e30)
    bias[...] = allowed

    def turn(x, r0, n):
        x = x.astype(F32)
        y = x * cs[pl.ds(r0, n), :] + pltpu.roll(x, D // 2, 1) * sn[pl.ds(r0, n), :]
        return y.astype(BF16)

    loads[1][1].wait()
    for h in range(KEY_VALUE_HEADS):
        kx[1, back:span, h * D:(h + 1) * D] = turn(ks[1, :, h * D:(h + 1) * D], 0, rows)
        send_key(1, h)
        if h + 1 < KEY_VALUE_HEADS:
            send_value(1, h + 1)
    loads[0][2].wait()
    loads[0][1].wait()
    for h in range(KEY_VALUE_HEADS):
        kx[0, back:span, h * D:(h + 1) * D] = turn(ks[0, :, h * D:(h + 1) * D], 0, rows)
        send_key(0, h)
        send_value(0, h)
    loads[1][0].wait()
    loads[0][0].wait()

    def arrived(p, h):
        there = kx.at[p, pl.ds(0, back), col(h)]
        pltpu.make_async_copy(there, there, k_recv.at[p, h]).wait()
        there = vx.at[p, pl.ds(0, back), col(h)]
        pltpu.make_async_copy(there, there, v_recv.at[p, h]).wait()

    factor = math.log2(math.e) / math.sqrt(D)
    keys = back + tile
    ones = jnp.ones((keys, D), BF16)

    def attend(p, h, head, t):
        q = turn(qs[p, t * tile:(t + 1) * tile, col(head)], t * tile, tile)
        k = kx[p, t * tile:t * tile + keys, col(h)]
        v = vx[p, t * tile:t * tile + keys, col(h)]
        x = lax.dot_general(q, k, (((1,), (1,)), ((), ())), preferred_element_type=F32)
        x = x * factor + bias[t * tile:(t + 1) * tile, t * tile:t * tile + keys]
        e = jnp.exp2(x - jnp.max(x, axis=1, keepdims=True)).astype(BF16)
        o = jnp.dot(e, jnp.concatenate([v, ones], axis=1), preferred_element_type=F32)
        return (o[:, :D] / o[:, D:]).astype(BF16)

    def move(src, dst, owner, send_sem, recv_sem):
        @pl.when(owner != me)
        def _():
            pltpu.make_async_remote_copy(
                src_ref=src, dst_ref=dst, send_sem=send_sem, recv_sem=recv_sem,
                device_id={"dp": owner}, device_id_type=MESH,
            ).start()

        @pl.when(owner == me)
        def _():
            pltpu.make_async_copy(src, dst, recv_sem).start()

    def drain(ref, sem):
        pltpu.make_async_copy(ref, ref, sem).wait()

    def base_group(h):
        arrived(0, h)

        def two_heads(i, c):
            for k in range(2):
                head = h * GROUP + 2 * i + k
                for t in range(rows // tile):
                    bo[t * tile:(t + 1) * tile, col(head)] = attend(0, h, head, t)
            return c

        lax.fori_loop(0, GROUP // 2, two_heads, 0)
        wide_col = pl.ds(pl.multiple_of(h * GROUP * D, GROUP * D), GROUP * D)
        pltpu.make_async_copy(bo.at[:, wide_col], base_out.at[:, wide_col], bo_sem).start()

    if cap is None:
        def actor_group(h, c):
            arrived(1, h)

            def one_head(i, c):
                j = lax.rem(me // splits + 1 + i, GROUP)
                for t in range(rows // tile):
                    att[h, j, t * tile:(t + 1) * tile, :] = attend(1, h, h * GROUP + j, t)
                for r in range(splits):
                    move(
                        att.at[h, j, pl.ds(r * part, part), :], land.at[h, me], j * splits + r,
                        one_send.at[h], one_recv.at[h],
                    )
                return c

            return lax.fori_loop(0, GROUP, one_head, c)

        my_rows = pl.ds(pl.multiple_of(lax.rem(me, splits) * part, part), part)

        def second_group(h, c):
            base_group(h)
            drain(land.at[h], one_recv.at[h])

            def one_group(i, c):
                g = lax.rem(me + 1 + i, owners)

                def pick(u, val):
                    return jnp.where(plan_ref[u] == g, land[h, u], val)

                fwd[h, g] = lax.fori_loop(1, owners, pick, land[h, 0], unroll=owners <= 8)
                move(
                    fwd.at[h, g], actor_out.at[my_rows, col(h * GROUP + me // splits)], g,
                    two_send.at[h], two_recv,
                )
                return c

            return lax.fori_loop(0, owners, one_group, c)

        moved = owners - 1
    else:
        half = owners // 2
        per = GROUP // half
        place_of = lax.rem(me, half)
        mine = me - place_of
        other = lax.rem(mine + half, owners)

        def ranks(first):
            taken, groups, out = 0, [], []
            for p in range(half):
                g = plan_ref[first + p]
                near = jnp.where(g >= first, 1, 0) * jnp.where(g < first + half, 1, 0)
                groups.append(g)
                out.append(jnp.where(near == 1, -1, taken))
                taken = taken + 1 - near
            return groups, out

        my_groups, my_ranks = ranks(mine)
        far_groups, far_ranks = ranks(other)

        def actor_piece(h, c):
            arrived(1, h)

            def one_piece(i, c):
                j = lax.rem(place_of + 1 + i, half)
                for k in range(per):
                    for t in range(rows // tile):
                        att[h, j, t * tile:(t + 1) * tile, k * D:(k + 1) * D] = attend(
                            1, h, h * GROUP + j * per + k, t
                        )
                move(att.at[h, j], land.at[h, place_of], mine + j, one_send.at[h], one_recv.at[h])
                return c

            lax.fori_loop(0, half, one_piece, 0)

            @pl.when(h >= 1)
            def _():
                cross(h - 1)

            return c

        def cross(h):
            drain(land.at[h], one_recv.at[h])
            for slot in range(cap):
                val = land[h, 0]
                for p in range(1, half):
                    val = jnp.where(my_ranks[p] == slot, land[h, p], val)
                out_box[h, slot] = val
            pltpu.make_async_remote_copy(
                src_ref=out_box.at[h], dst_ref=in_box.at[h],
                send_sem=box_send.at[h], recv_sem=box_recv.at[h],
                device_id={"dp": lax.rem(me + half, owners)}, device_id_type=MESH,
            ).start()

        wide = per * D
        actor_group = actor_piece

        def second_group(h, c):
            base_group(h)

            @pl.when(h == 0)
            def _():
                cross(KEY_VALUE_HEADS - 1)

            drain(in_box.at[h], box_recv.at[h])

            def one_group(i, c):
                r = lax.rem(place_of + 1 + i, half)
                g = mine + r
                val = land[h, 0]
                for p in range(1, half):
                    val = jnp.where(my_groups[p] == g, land[h, p], val)
                for slot in range(cap):
                    hit = 0
                    for p in range(half):
                        hit = hit + jnp.where(far_groups[p] == g, 1, 0) * jnp.where(
                            far_ranks[p] == slot, 1, 0
                        )
                    val = jnp.where(hit == 1, in_box[h, slot], val)
                fwd[h, r] = val
                there = pl.ds(pl.multiple_of((h * half + place_of) * wide, wide), wide)
                move(fwd.at[h, r], actor_out.at[:, there], g, two_send.at[h], two_recv)
                return c

            return lax.fori_loop(0, half, one_group, c)

        moved = half - 1

    lax.fori_loop(0, KEY_VALUE_HEADS, actor_group, 0)
    lax.fori_loop(0, KEY_VALUE_HEADS, second_group, 0)

    drain(labs.at[pl.ds(0, 2)], lab_send)
    for p in range(2):
        drain(kx.at[p, pl.ds(0, back), :], k_send.at[p])
        drain(vx.at[p, pl.ds(0, back), :], v_send.at[p])
    for h in range(KEY_VALUE_HEADS):
        drain(land.at[h, pl.ds(0, moved)], one_send.at[h])
    drain(base_out, bo_sem)
    for h in range(KEY_VALUE_HEADS):
        drain(land.at[h, pl.ds(0, moved)], two_send.at[h])
        if cap is not None:
            drain(out_box.at[h], box_send.at[h])
    drain(actor_out, two_recv)


def per_device(owners, members, bq, bk, bv, aq, ak, av, labels, plan):
    rows = bq.shape[1]
    width = bq.shape[2]
    narrow = bk.shape[2]
    D = HEAD_SIZE
    half = np.arange(D) % (D // 2)
    rates = np.exp(half.astype(np.float64) * (-2.0 * math.log(THETA) / D)).astype(np.float32)
    rates = jnp.asarray(np.broadcast_to(rates, (8, D)))
    vmem = pl.BlockSpec(memory_space=pltpu.VMEM)
    hbm = pl.BlockSpec(memory_space=pl.ANY)
    out = jax.ShapeDtypeStruct((rows, width), BF16)
    dma = pltpu.SemaphoreType.DMA
    KV = KEY_VALUE_HEADS

    def call(cap, number, *args):
        if cap is None:
            part = (owners, rows // (owners // GROUP), D)
            made = (GROUP, rows, D)
            box = (1, 1, 16, D)
        else:
            part = made = (owners // 2, rows, GROUP // (owners // 2) * D)
            box = (KV, cap) + part[1:]
        return pl.pallas_call(
            functools.partial(kernel, owners, members, rows, rows // 2, cap),
            out_shape=(out, out),
            in_specs=[pl.BlockSpec(memory_space=pltpu.SMEM)] + [vmem] * 2 + [hbm] * 6,
            out_specs=(hbm, hbm),
            scratch_shapes=[
                pltpu.VMEM((3, 8, rows), jnp.int32),
                pltpu.VMEM((rows, D), F32),
                pltpu.VMEM((rows, D), F32),
                pltpu.VMEM((rows, 3 * rows), F32),
                pltpu.VMEM((2, rows, width), BF16),
                pltpu.VMEM((2, rows, narrow), BF16),
                pltpu.VMEM((2, 3 * rows, narrow), BF16),
                pltpu.VMEM((2, 3 * rows, narrow), BF16),
                pltpu.VMEM((KV,) + made, BF16),
                pltpu.VMEM((KV,) + part, BF16),
                pltpu.VMEM((KV,) + part, BF16),
                pltpu.VMEM((rows, width), BF16),
                pltpu.VMEM(box, BF16),
                pltpu.VMEM(box, BF16),
                dma((2,)), dma((2,)), dma((2,)),
                dma, dma, dma((2,)), dma((2,)), dma((2, KV)), dma((2, KV)),
                dma((KV,)), dma((KV,)), dma((KV,)), dma, dma, dma((KV,)), dma((KV,)),
            ],
            compiler_params=pltpu.CompilerParams(
                collective_id=number, has_side_effects=True, vmem_limit_bytes=60 * 1024 * 1024
            ),
            cost_estimate=pl.CostEstimate(
                flops=2 * 4 * rows * (5 * rows // 2) * width, bytes_accessed=8 * rows * width,
                transcendentals=0,
            ),
        )(*args)

    args = (plan, labels, rates, bq[0], bk[0], bv[0], aq[0], ak[0], av[0])
    if owners != 8:
        base, actor = call(None, 0, *args)
    else:
        leaving = jnp.sum((plan[: owners // 2] >= owners // 2).astype(jnp.int32))
        caps = range(1, owners // 2 + 1)
        base, actor = lax.switch(
            jnp.maximum(leaving, 1) - 1,
            [functools.partial(call, cap, cap) for cap in caps],
            *args,
        )
    return base[None], actor[None]


def solution(mesh):
    rows3 = P("dp", "sp", None)
    return jax.shard_map(
        functools.partial(per_device, mesh.shape["dp"], mesh.shape["sp"]),
        mesh=mesh,
        in_specs=(rows3,) * 6 + (P("dp", "sp"), P()),
        out_specs=(rows3, rows3),
        check_vma=False,
    )
```

profile of v0, /device:TPU:0, one launch (start us, length us, event | category | flops | bytes accessed | tf_op | source)
XLA Modules:
  0.0 89.8 jit_solution(13747380878078768842)
XLA Ops:
  0.6 1.3 %fusion = s32[]{:T(128)} fusion(s32[8]{0:T(128)} %param.20), kind=kLoop, calls=%fused_computation.1 | loop fusion | flops 11 | bytes 20 | tf_op jit(solution)/shard_map/reduce_sum | solution.py:391
  2.6 0.7 jit_solution_.3
  3.2 82.9 %conditional.1 = ((bf16[256,4096]{1,0:T(8,128)(2,1)S(1)}, bf16[256,4096]{1,0:T(8,128)(2,1)})) conditional(s32[]{:T(128)} %clamp.3, (s32[8]{0:T(128)}, s32[1,256]{1,0:T(1,128)}, f32[8,128]{1,0:T(8,128)S(1)}, bf16[256,4096]{1,0:T(8,128)(2,1)}, bf16[256,512]{1,0:T(8,128)(2,1)}, /*index=5*/bf16[256,512]{1,0:T(8,128)(2,1)}, ...), branch_computations={%region_1.0_spmd, %region_2.0_spmd, %region_3.0_spmd, %region_4.0_... | conditional | flops 5368709120 | bytes 8388616 | solution.py:393
  3.2 82.7 %branch_1_fun.1 = (bf16[256,4096]{1,0:T(8,128)(2,1)S(1)}, bf16[256,4096]{1,0:T(8,128)(2,1)}) custom-call(s32[8]{0:T(128)} %get-tuple-element.93.plan_ref, s32[1,256]{1,0:T(1,128)} %get-tuple-element.94.lab_ref, f32[8,128]{1,0:T(8,128)S(1)} %get-tuple-element.95.rate_ref, bf16[256,4096]{1,0:T(8,128)(2,1)} %get-tuple-element.96.bq_hbm, ...), custom_call_target="tpu_custom_call" | custom-call | flops 5368709120 | bytes 8388608 | tf_op jit(solution)/shard_map/cond/branch_1_fun/pallas_call | solution.py:354
  86.1 0.0 copy-start
  86.2 1.3 %copy.21 = bf16[1,256,4096]{2,1,0:T(8,128)(2,1)} copy(bf16[1,256,4096]{2,1,0:T(8,128)(2,1)S(1)} %bitcast.8) | data formatting | bytes 4194304
  87.5 1.0 %copy-done = bf16[256,4096]{1,0:T(8,128)(2,1)S(1)} copy-done((bf16[256,4096]{1,0:T(8,128)(2,1)S(1)}, bf16[256,4096]{1,0:T(8,128)(2,1)}, u32[]{:S(2)}) %copy-start) | copy-done | bytes 2097176
  88.5 1.3 %copy.22 = bf16[1,256,4096]{2,1,0:T(8,128)(2,1)} copy(bf16[1,256,4096]{2,1,0:T(8,128)(2,1)S(1)} %bitcast.9) | data formatting | bytes 4194304
Async XLA Ops:
  86.1 2.3 %copy-start = (bf16[256,4096]{1,0:T(8,128)(2,1)S(1)}, bf16[256,4096]{1,0:T(8,128)(2,1)}, u32[]{:S(2)}) copy-start(bf16[256,4096]{1,0:T(8,128)(2,1)} %get-tuple-element.129) | copy-start | bytes 6291460
where the time goes:
time: 90 us; the launch traced here: 89.8 us
  Pallas kernels  82.7 us (92%)
  local copies, waits for them, and re-layouts  4.32 us (5%)
  between operations  1.3 us (1%)
  other arithmetic  1.29 us (1%)
    pallas_call x1, Pallas kernels, call(): pl.pallas_call(functools.partial(kernel, owners, members, rows, rows // 2...  82.7 us
    unnamed x4, local copies, waits for them, and re-layouts  3.66 us

commit v1 on v0

--- a/solution.py
+++ b/solution.py
@@ -23,10 +23,10 @@
     owners, members, rows, tile, cap,
     plan_ref, lab_ref, rate_ref, bq_hbm, bk_hbm, bv_hbm, aq_hbm, ak_hbm, av_hbm,
     base_out, actor_out,
-    labs, cs, sn, bias, qs, ks, kx, vx, att, land, fwd, bo, out_box, in_box,
+    labs, cs, sn, bias, qs, ks, kx, vx, att, land, fwd, bo, out_box, in_box, fin,
     q_sem, k_sem, v_sem,
     lab_send, lab_recv, k_send, v_send, k_recv, v_recv,
-    one_send, one_recv, two_send, two_recv, bo_sem, box_send, box_recv,
+    one_send, one_recv, two_send, two_recv, bo_sem, box_send, box_recv, fin_sem,
 ):
     D = HEAD_SIZE
     me = lax.axis_index("dp")
@@ -41,10 +41,15 @@
         loads[p] = (
             pltpu.make_async_copy(q_hbm, qs.at[p], q_sem.at[p]),
             pltpu.make_async_copy(k_hbm, ks.at[p], k_sem.at[p]),
-            pltpu.make_async_copy(v_hbm, vx.at[p, pl.ds(back, rows), :], v_sem.at[p]),
+            [
+                pltpu.make_async_copy(
+                    v_hbm.at[:, pl.ds(h * D, D)], vx.at[p, h, pl.ds(back, rows)], v_sem.at[p, h]
+                )
+                for h in range(KEY_VALUE_HEADS)
+            ],
         )
     for p in (1, 0):
-        for load in (loads[p][2], loads[p][1], loads[p][0]):
+        for load in loads[p][2] + [loads[p][1], loads[p][0]]:
             load.start()
 
     def col(h):
@@ -79,20 +84,20 @@
 
     def send_key(p, h):
         to_later(
-            kx.at[p, pl.ds(back, rows), col(h)],
-            lambda slot: kx.at[p, pl.ds(slot * rows, rows), col(h)],
+            kx.at[p, h, pl.ds(back, rows)],
+            lambda slot: kx.at[p, h, pl.ds(slot * rows, rows)],
             k_send.at[p], k_recv.at[p, h],
         )
 
     def send_value(p, h):
+        loads[p][2][h].wait()
         to_later(
-            vx.at[p, pl.ds(back, rows), col(h)],
-            lambda slot: vx.at[p, pl.ds(slot * rows, rows), col(h)],
+            vx.at[p, h, pl.ds(back, rows)],
+            lambda slot: vx.at[p, h, pl.ds(slot * rows, rows)],
             v_send.at[p], v_recv.at[p, h],
         )
 
     to_later(labs.at[2], lambda slot: labs.at[slot], lab_send, lab_recv)
-    loads[1][2].wait()
     send_value(1, 0)
     pltpu.make_async_copy(labs.at[pl.ds(0, 2)], labs.at[pl.ds(0, 2)], lab_recv).wait()
 
@@ -106,7 +111,7 @@
     begin = jnp.sum(jnp.where(lab_row < lab_col, 1.0, 0.0), axis=1, keepdims=True)
     r_place = lax.broadcasted_iota(jnp.int32, (rows, 1), 0) + back
     positions = r_place.astype(F32) - begin
-    angles = positions * rate_ref[:1, :]
+    angles = positions * rate_ref[...]
     lane = lax.broadcasted_iota(jnp.int32, (rows, D), 1)
     cs[...] = jnp.cos(angles)
     sine = jnp.sin(angles)
@@ -123,23 +128,21 @@
 
     loads[1][1].wait()
     for h in range(KEY_VALUE_HEADS):
-        kx[1, back:span, h * D:(h + 1) * D] = turn(ks[1, :, h * D:(h + 1) * D], 0, rows)
+        kx[1, h, back:span, :] = turn(ks[1, :, h * D:(h + 1) * D], 0, rows)
         send_key(1, h)
         if h + 1 < KEY_VALUE_HEADS:
             send_value(1, h + 1)
-    loads[0][2].wait()
     loads[0][1].wait()
     for h in range(KEY_VALUE_HEADS):
-        kx[0, back:span, h * D:(h + 1) * D] = turn(ks[0, :, h * D:(h + 1) * D], 0, rows)
+        kx[0, h, back:span, :] = turn(ks[0, :, h * D:(h + 1) * D], 0, rows)
         send_key(0, h)
         send_value(0, h)
     loads[1][0].wait()
-    loads[0][0].wait()
 
     def arrived(p, h):
-        there = kx.at[p, pl.ds(0, back), col(h)]
+        there = kx.at[p, h, pl.ds(0, back)]
         pltpu.make_async_copy(there, there, k_recv.at[p, h]).wait()
-        there = vx.at[p, pl.ds(0, back), col(h)]
+        there = vx.at[p, h, pl.ds(0, back)]
         pltpu.make_async_copy(there, there, v_recv.at[p, h]).wait()
 
     factor = math.log2(math.e) / math.sqrt(D)
@@ -148,8 +151,8 @@
 
     def attend(p, h, head, t):
         q = turn(qs[p, t * tile:(t + 1) * tile, col(head)], t * tile, tile)
-        k = kx[p, t * tile:t * tile + keys, col(h)]
-        v = vx[p, t * tile:t * tile + keys, col(h)]
+        k = kx[p, h, t * tile:t * tile + keys, :]
+        v = vx[p, h, t * tile:t * tile + keys, :]
         x = lax.dot_general(q, k, (((1,), (1,)), ((), ())), preferred_element_type=F32)
         x = x * factor + bias[t * tile:(t + 1) * tile, t * tile:t * tile + keys]
         e = jnp.exp2(x - jnp.max(x, axis=1, keepdims=True)).astype(BF16)
@@ -217,7 +220,7 @@
                 fwd[h, g] = lax.fori_loop(1, owners, pick, land[h, 0], unroll=owners <= 8)
                 move(
                     fwd.at[h, g], actor_out.at[my_rows, col(h * GROUP + me // splits)], g,
-                    two_send.at[h], two_recv,
+                    two_send.at[h], fin_sem,
                 )
                 return c
 
@@ -304,8 +307,7 @@
                         )
                     val = jnp.where(hit == 1, in_box[h, slot], val)
                 fwd[h, r] = val
-                there = pl.ds(pl.multiple_of((h * half + place_of) * wide, wide), wide)
-                move(fwd.at[h, r], actor_out.at[:, there], g, two_send.at[h], two_recv)
+                move(fwd.at[h, r], fin.at[h, place_of], g, two_send.at[h], two_recv.at[h])
                 return c
 
             return lax.fori_loop(0, half, one_group, c)
@@ -313,12 +315,20 @@
         moved = half - 1
 
     lax.fori_loop(0, KEY_VALUE_HEADS, actor_group, 0)
+    loads[0][0].wait()
     lax.fori_loop(0, KEY_VALUE_HEADS, second_group, 0)
+
+    if cap is not None:
+        for h in range(KEY_VALUE_HEADS):
+            drain(fin.at[h], two_recv.at[h])
+            for p in range(half):
+                there = pl.ds((h * half + p) * wide, wide)
+                pltpu.make_async_copy(fin.at[h, p], actor_out.at[:, there], fin_sem).start()
 
     drain(labs.at[pl.ds(0, 2)], lab_send)
     for p in range(2):
-        drain(kx.at[p, pl.ds(0, back), :], k_send.at[p])
-        drain(vx.at[p, pl.ds(0, back), :], v_send.at[p])
+        drain(kx.at[p, :, pl.ds(0, back), :], k_send.at[p])
+        drain(vx.at[p, :, pl.ds(0, back), :], v_send.at[p])
     for h in range(KEY_VALUE_HEADS):
         drain(land.at[h, pl.ds(0, moved)], one_send.at[h])
     drain(base_out, bo_sem)
@@ -326,7 +336,7 @@
         drain(land.at[h, pl.ds(0, moved)], two_send.at[h])
         if cap is not None:
             drain(out_box.at[h], box_send.at[h])
-    drain(actor_out, two_recv)
+    drain(actor_out, fin_sem)
 
 
 def per_device(owners, members, bq, bk, bv, aq, ak, av, labels, plan):
@@ -336,7 +346,7 @@
     D = HEAD_SIZE
     half = np.arange(D) % (D // 2)
     rates = np.exp(half.astype(np.float64) * (-2.0 * math.log(THETA) / D)).astype(np.float32)
-    rates = jnp.asarray(np.broadcast_to(rates, (8, D)))
+    rates = jnp.asarray(rates.reshape(1, D))
     vmem = pl.BlockSpec(memory_space=pltpu.VMEM)
     hbm = pl.BlockSpec(memory_space=pl.ANY)
     out = jax.ShapeDtypeStruct((rows, width), BF16)
@@ -363,17 +373,18 @@
                 pltpu.VMEM((rows, 3 * rows), F32),
                 pltpu.VMEM((2, rows, width), BF16),
                 pltpu.VMEM((2, rows, narrow), BF16),
-                pltpu.VMEM((2, 3 * rows, narrow), BF16),
-                pltpu.VMEM((2, 3 * rows, narrow), BF16),
+                pltpu.VMEM((2, KV, 3 * rows, D), BF16),
+                pltpu.VMEM((2, KV, 3 * rows, D), BF16),
                 pltpu.VMEM((KV,) + made, BF16),
                 pltpu.VMEM((KV,) + part, BF16),
                 pltpu.VMEM((KV,) + part, BF16),
                 pltpu.VMEM((rows, width), BF16),
                 pltpu.VMEM(box, BF16),
                 pltpu.VMEM(box, BF16),
-                dma((2,)), dma((2,)), dma((2,)),
+                pltpu.VMEM((KV,) + part if cap else (1, 1, 16, D), BF16),
+                dma((2,)), dma((2,)), dma((2, KV)),
                 dma, dma, dma((2,)), dma((2,)), dma((2, KV)), dma((2, KV)),
-                dma((KV,)), dma((KV,)), dma((KV,)), dma, dma, dma((KV,)), dma((KV,)),
+                dma((KV,)), dma((KV,)), dma((KV,)), dma((KV,)), dma, dma((KV,)), dma((KV,)), dma,
             ],
             compiler_params=pltpu.CompilerParams(
                 collective_id=number, has_side_effects=True, vmem_limit_bytes=60 * 1024 * 1024

time: 90 us -> 89.8 us (level)
  no operation moved by 1% of the time
where the time goes in v1:
time: 89.8 us; the launch traced here: 89.6 us
  Pallas kernels  83.1 us (93%)
  local copies, waits for them, and re-layouts  3.66 us (4%)
  between operations  1.3 us (1%)
  other arithmetic  1.29 us (1%)
    pallas_call x1, Pallas kernels, call(): pl.pallas_call(functools.partial(kernel, owners, members, rows, rows // 2...  83.1 us
    unnamed x4, local copies, waits for them, and re-layouts  3.66 us

profile of v1, /device:TPU:0, one launch (start us, length us, event | category | flops | bytes accessed | tf_op | source)
XLA Modules:
  0.0 89.6 jit_solution(11821474530167081741)
XLA Ops:
  0.6 1.3 %fusion = s32[]{:T(128)} fusion(s32[8]{0:T(128)} %param.20), kind=kLoop, calls=%fused_computation.1 | loop fusion | flops 11 | bytes 20 | tf_op jit(solution)/shard_map/reduce_sum | solution.py:402
  2.6 83.3 %conditional.1 = ((bf16[256,4096]{1,0:T(8,128)(2,1)S(1)}, bf16[256,4096]{1,0:T(8,128)(2,1)})) conditional(s32[]{:T(128)} %clamp.3, (s32[8]{0:T(128)}, s32[1,256]{1,0:T(1,128)}, f32[1,128]{1,0:T(1,128)}, bf16[256,4096]{1,0:T(8,128)(2,1)}, bf16[256,512]{1,0:T(8,128)(2,1)}, /*index=5*/bf16[256,512]{1,0:T(8,128)(2,1)}, ...), branch_computations={%region_1.0_spmd, %region_2.0_spmd, %region_3.0_spmd, %region_4.0_... | conditional | flops 5368709120 | bytes 8388616 | solution.py:404
  2.6 83.1 %branch_1_fun.1 = (bf16[256,4096]{1,0:T(8,128)(2,1)S(1)}, bf16[256,4096]{1,0:T(8,128)(2,1)}) custom-call(s32[8]{0:T(128)} %get-tuple-element.93.plan_ref, s32[1,256]{1,0:T(1,128)} %get-tuple-element.94.lab_ref, f32[1,128]{1,0:T(1,128)} %get-tuple-element.95.rate_ref, bf16[256,4096]{1,0:T(8,128)(2,1)} %get-tuple-element.96.bq_hbm, ...), custom_call_target="tpu_custom_call" | custom-call | flops 5368709120 | bytes 8388608 | tf_op jit(solution)/shard_map/cond/branch_1_fun/pallas_call | solution.py:364
  85.9 0.0 copy-start
  85.9 1.3 %copy.21 = bf16[1,256,4096]{2,1,0:T(8,128)(2,1)} copy(bf16[1,256,4096]{2,1,0:T(8,128)(2,1)S(1)} %bitcast.8) | data formatting | bytes 4194304
  87.3 1.0 %copy-done = bf16[256,4096]{1,0:T(8,128)(2,1)S(1)} copy-done((bf16[256,4096]{1,0:T(8,128)(2,1)S(1)}, bf16[256,4096]{1,0:T(8,128)(2,1)}, u32[]{:S(2)}) %copy-start) | copy-done | bytes 2097176
  88.3 1.3 %copy.22 = bf16[1,256,4096]{2,1,0:T(8,128)(2,1)} copy(bf16[1,256,4096]{2,1,0:T(8,128)(2,1)S(1)} %bitcast.9) | data formatting | bytes 4194304
Async XLA Ops:
  85.9 2.3 %copy-start = (bf16[256,4096]{1,0:T(8,128)(2,1)S(1)}, bf16[256,4096]{1,0:T(8,128)(2,1)}, u32[]{:S(2)}) copy-start(bf16[256,4096]{1,0:T(8,128)(2,1)} %get-tuple-element.129) | copy-start | bytes 6291460
